TPU v7x, 32 devices: a whole 2x2x4 slice. The times are simulated.
32 devices in a mesh: dp: 32 (over z, y, x, core).
Axes of the slice: x: 2, y: 2, z: 4, core: 2. Of those that a mesh axis runs over, the one named last changes fastest.
Arguments:
- inputs: bfloat16 [31520, 384], P('dp'), may hold values from -6 to 6
- weights: bfloat16 [13824, 128], P('dp'), may hold values from -0.8164966 to 0.8164966
- vectors: float32 [36, 128], replicated, may hold values from -2 to 2
- cotangent: bfloat16 [31520, 384], P('dp'), may hold values from -6 to 6
- mom_weights: float32 [13824, 128], P('dp'), may hold values from -213.046474 to 213.046474
- mom_vectors: float32 [36, 128], replicated, may hold values from -355.07746 to 355.07746
Outputs:
- output: bfloat16 [31520, 384], P('dp')
- grad_inputs: float32 [31520, 384], P('dp')
- grad_weights: float32 [13824, 128], P('dp')
- grad_vectors: float32 [36, 128], replicated
- new_mom_weights: float32 [13824, 128], P('dp')
- new_mom_vectors: float32 [36, 128], replicated
- update_weights: float32 [13824, 128], P('dp')
- update_vectors: float32 [36, 128], replicated
All inputs are finite; a program needn't handle non-finite values.
Results may differ from a plain program's by a relative error of at most 0.012.
Values may be sent and summed in bfloat16 or wider, within the bound.
A program may use at most 128 MiB of HBM per device.

v0:
```python
import math
import jax
import jax.numpy as jnp
from jax import lax
from jax.sharding import PartitionSpec as P

D = 384
HEADS = 6
HD = 64
FF = 1536
SEQ = 197
HIGH = lax.Precision.HIGHEST
MOMENTUM = 0.95
MATRIX_RATE = 0.5
VECTOR_RATE = 0.2
NEWTON_COEFFS = (3.4445, -4.775, 2.0315)
NORM_EPS = 1e-06


def split_matrices(flat):
    flat_line = flat.reshape(-1)
    layout = ((D, 3 * D), (D, D), (D, FF), (FF, D))
    pieces = []
    offset = 0
    for dims_pair in layout:
        entries = dims_pair[0] * dims_pair[1]
        pieces.append(flat_line[offset : offset + entries].reshape(dims_pair))
        offset = offset + entries
    return pieces


def split_vectors(flat):
    flat_line = flat.reshape(-1)
    pieces = []
    offset = 0
    for length_one in (D, D, D, D, D, D, D, D, FF):
        pieces.append(flat_line[offset : offset + length_one])
        offset = offset + length_one
    return pieces


def layer_norm(value, norm_gain, norm_shift):
    center = jnp.mean(value, axis=-1, keepdims=True)
    deviation = value - center
    spread = jnp.mean(deviation * deviation, axis=-1, keepdims=True)
    return deviation * lax.rsqrt(spread + NORM_EPS) * norm_gain + norm_shift


def gelu_exact(value):
    return jax.nn.gelu(value, approximate=False)


def matmul(left, right):
    return jnp.dot(left, right, preferred_element_type=jnp.float32)


def outer_sum(left, right):
    return lax.dot_general(
        left, right, (((0,), (0,)), ((), ())), preferred_element_type=jnp.float32
    )


def times_transpose(left, right):
    return lax.dot_general(
        left, right, (((1,), (1,)), ((), ())), preferred_element_type=jnp.float32
    )


def column_sums(value):
    return jnp.sum(value.astype(jnp.float32), axis=0)


def orthogonalize(matrix):
    tall = matrix.shape[0] > matrix.shape[1]
    current = matrix.T if tall else matrix
    current = current / (jnp.sqrt(jnp.sum(current * current)) + 1e-07)
    first, second, third = NEWTON_COEFFS
    for repeat in range(5):
        square = jnp.dot(current, current.T, precision=HIGH)
        poly = second * square + third * jnp.dot(square, square, precision=HIGH)
        current = first * current + jnp.dot(poly, current, precision=HIGH)
    return current.T if tall else current


def blank_like(matrix):
    return jnp.zeros_like(matrix)


def on_device(inputs, weights, vectors, cotangent, mom_weights, mom_vectors):
    count = lax.axis_size("dp")
    device_index = lax.axis_index("dp")
    whole = lax.all_gather(weights, "dp", axis=0, tiled=True)
    w_qkv, w_out, w_up, w_down = split_matrices(whole)
    ln1_gain, ln1_shift, bias_q, bias_v, bias_out, ln2_gain, ln2_shift, bias_down, bias_up = (
        split_vectors(vectors)
    )
    rows = inputs.shape[0]
    images = rows // SEQ
    scale_qk = HD ** (-0.5)
    residual_in = inputs.astype(jnp.float32)
    normed, norm_pull = jax.vjp(layer_norm, residual_in, ln1_gain, ln1_shift)
    normed_low = normed.astype(jnp.bfloat16)
    bias_qkv = jnp.concatenate([bias_q, jnp.zeros_like(bias_q), bias_v])
    qkv = (
        (matmul(normed_low, w_qkv) + bias_qkv)
        .astype(jnp.bfloat16)
        .reshape(images, SEQ, 3, HEADS, HD)
    )
    queries = qkv[:, :, 0]
    key_rows = qkv[:, :, 1]
    values = qkv[:, :, 2]
    scores = (
        jnp.einsum("bqhd,bkhd->bhqk", queries, key_rows, preferred_element_type=jnp.float32)
        * scale_qk
    )
    row_max = jnp.max(scores, axis=-1, keepdims=True)
    log_total = row_max + jnp.log(jnp.sum(jnp.exp(scores - row_max), axis=-1, keepdims=True))
    probs_low = jnp.exp(scores - log_total).astype(jnp.bfloat16)
    attended = jnp.einsum("bhqk,bkhd->bqhd", probs_low, values, preferred_element_type=jnp.float32)
    attended = attended.reshape(rows, D).astype(jnp.bfloat16)
    middle = residual_in + matmul(attended, w_out) + bias_out
    normed_two, norm_pull_two = jax.vjp(layer_norm, middle, ln2_gain, ln2_shift)
    normed_two_low = normed_two.astype(jnp.bfloat16)
    hidden = matmul(normed_two_low, w_up) + bias_up
    unused_out, gelu_pull = jax.vjp(gelu_exact, hidden)
    active = gelu_exact(hidden).astype(jnp.bfloat16)
    result = middle + matmul(active, w_down) + bias_down
    output = result.astype(jnp.bfloat16)
    again = lax.all_gather(weights, "dp", axis=0, tiled=True)
    w_qkv, w_out, w_up, w_down = split_matrices(again)
    grad_down = outer_sum(active, cotangent)
    grad_bias_down = column_sums(cotangent)
    d_active = times_transpose(cotangent, w_down)
    d_hidden = gelu_pull(d_active)[0].astype(jnp.bfloat16)
    grad_up = outer_sum(normed_two_low, d_hidden)
    grad_bias_up = column_sums(d_hidden)
    d_normed_two = times_transpose(d_hidden, w_up)
    d_middle_norm, grad_ln2_gain, grad_ln2_shift = norm_pull_two(d_normed_two)
    d_middle = cotangent.astype(jnp.float32) + d_middle_norm
    d_branch = d_middle.astype(jnp.bfloat16)
    grad_out = outer_sum(attended, d_branch)
    grad_bias_out = column_sums(d_branch)
    d_attended = (
        times_transpose(d_branch, w_out).astype(jnp.bfloat16).reshape(images, SEQ, HEADS, HD)
    )
    scores_again = (
        jnp.einsum("bqhd,bkhd->bhqk", queries, key_rows, preferred_element_type=jnp.float32)
        * scale_qk
    )
    probs_full = jnp.exp(scores_again - log_total)
    probs_again = probs_full.astype(jnp.bfloat16)
    grad_values = jnp.einsum(
        "bhqk,bqhd->bkhd", probs_again, d_attended, preferred_element_type=jnp.float32
    )
    d_probs = jnp.einsum("bqhd,bkhd->bhqk", d_attended, values, preferred_element_type=jnp.float32)
    d_scores = probs_full * (d_probs - jnp.sum(d_probs * probs_full, axis=-1, keepdims=True))
    d_scores = d_scores.astype(jnp.bfloat16)
    grad_queries = (
        jnp.einsum("bhqk,bkhd->bqhd", d_scores, key_rows, preferred_element_type=jnp.float32)
        * scale_qk
    )
    grad_keys = (
        jnp.einsum("bhqk,bqhd->bkhd", d_scores, queries, preferred_element_type=jnp.float32)
        * scale_qk
    )
    d_qkv = (
        jnp.stack([grad_queries, grad_keys, grad_values], axis=2)
        .astype(jnp.bfloat16)
        .reshape(rows, 3 * D)
    )
    grad_qkv = outer_sum(normed_low, d_qkv)
    grad_bias_q = column_sums(d_qkv[:, :D])
    grad_bias_v = column_sums(d_qkv[:, 2 * D :])
    d_normed = times_transpose(d_qkv, w_qkv)
    d_input_norm, grad_ln1_gain, grad_ln1_shift = norm_pull(d_normed)
    grad_inputs = d_middle + d_input_norm
    local_grads = jnp.concatenate(
        [grad_qkv.reshape(-1), grad_out.reshape(-1), grad_up.reshape(-1), grad_down.reshape(-1)]
    )
    local_grads = local_grads.reshape(-1, 128)
    local_vector_grads = jnp.concatenate(
        [
            grad_ln1_gain,
            grad_ln1_shift,
            grad_bias_q,
            grad_bias_v,
            grad_bias_out,
            grad_ln2_gain,
            grad_ln2_shift,
            grad_bias_down,
            grad_bias_up,
        ]
    ).reshape(-1, 128)
    grad_vectors = lax.psum(local_vector_grads, "dp")
    grad_weights = lax.psum_scatter(local_grads, "dp", scatter_dimension=0, tiled=True)
    new_mom_weights = MOMENTUM * mom_weights + grad_weights
    gathered = lax.all_gather(new_mom_weights, "dp", axis=0, tiled=True)
    new_mom_vectors = MOMENTUM * mom_vectors + grad_vectors
    mom_matrices = split_matrices(gathered)
    owned_list = []
    for matrix_slot in range(4):
        owner_rank = 0
        computed = lax.cond(
            device_index == owner_rank, orthogonalize, blank_like, mom_matrices[matrix_slot]
        )
        owned_list.append(computed)
    owned_flat = jnp.concatenate([item.reshape(-1) for item in owned_list]).reshape(-1, 128)
    own_rows = lax.psum_scatter(owned_flat, "dp", scatter_dimension=0, tiled=True)
    update_weights = -MATRIX_RATE * own_rows
    total_tokens = rows * count
    update_vectors = -(VECTOR_RATE / math.sqrt(total_tokens)) * new_mom_vectors
    return (
        output,
        grad_inputs,
        grad_weights,
        grad_vectors,
        new_mom_weights,
        new_mom_vectors,
        update_weights,
        update_vectors,
    )


def solution(mesh):
    in_specs = (P("dp", None), P("dp", None), P(), P("dp", None), P("dp", None), P())
    out_specs = (
        P("dp", None),
        P("dp", None),
        P("dp", None),
        P(),
        P("dp", None),
        P(),
        P("dp", None),
        P(),
    )
    return jax.shard_map(
        on_device, mesh=mesh, in_specs=in_specs, out_specs=out_specs, check_vma=False
    )
```

profile of v0, /device:TPU:0, one launch (start us, length us, event | category | flops | bytes accessed | tf_op | source)
XLA Modules:
  0.0 743.2 jit_solution(9406631774744465408)
XLA Ops:
  14.8 58.9 %all-gather.3.cloned.1.call-done = bf16[13824,128]{1,0:T(8,128)(2,1)} async-done(((bf16[432,128]{1,0:T(8,128)(2,1)}), bf16[13824,128]{1,0:T(8,128)(2,1)}) %all-gather.3.cloned.1.call-update) | async-done | bytes 3538960 | tf_op jit(solution)/shard_map/all_gather | solution.py:92
  85.0 5.7 reshape.262
  90.7 5.8 fusion.79
  115.7 15.7 %multiply_convert_fusion.1 = (bf16[985,1536]{1,0:T(8,128)(2,1)}, f32[985,1536]{1,0:T(8,128)S(1)}, f32[985,1536]{1,0:T(8,128)S(1)}) fusion(f32[1536]{0:T(1024)S(1)} %copy-done.31, bf16[384,1536]{1,0:T(8,128)(2,1)S(1)} %copy-done.24, f32[985,384]{1,0:T(8,128)S(1)} %get-tuple-element.75, f32[384]{0:T(512)S(1)} %copy-done.36, f32[384]{0:T(512)S(1)} %get-tuple-element.66, ...), kind=kOutput, calls=%fused_computation.96 | convolution fusion | flops 1263699840 | bytes 17839304 | tf_op jit(solution)/shard_map/dot_general | solution.py:54
  149.9 5.4 convolution_bitcast_fusion
  177.2 4.5 copy.40
  181.7 7.6 %convert_element_type.97 = bf16[985,1152]{0,1:T(8,128)(2,1)} reshape(bf16[5,197,3,6,64]{1,0,4,3,2:T(8,128)(2,1)} %copy.40) | data formatting | bytes 4538880 | tf_op jit(solution)/shard_map/convert_element_type | solution.py:168
  196.2 8.8 %maximum_bitcast_fusion = f32[13824,128]{1,0:T(8,128)} fusion(f32[589824]{0:T(1024)S(1)} %reshape.258, f32[589824]{0:T(1024)} %reshape.257, f32[147456]{0:T(1024)} %reshape.256, f32[442368]{0:T(1024)} %reshape.255), kind=kLoop, calls=%fused_computation.87 | loop fusion | flops 5308416 | bytes 14155776 | tf_op jit(solution)/shard_map/reshape | solution.py:180
  205.1 118.2 %reduce-scatter.3.cloned.1.call-done = f32[432,128]{1,0:T(8,128)} async-done(((f32[13824,128]{1,0:T(8,128)}), f32[432,128]{1,0:T(8,128)}) %reduce-scatter.3.cloned.1.call-update) | async-done | bytes 221200 | tf_op jit(solution)/shard_map/reduce_scatter | solution.py:195
  325.0 73.9 %all-gather.5.cloned.1.call-done = f32[13824,128]{1,0:T(8,128)} async-done(((f32[432,128]{1,0:T(8,128)}), f32[13824,128]{1,0:T(8,128)}) %all-gather.5.cloned.1.call-update) | async-done | bytes 7077904 | tf_op jit(solution)/shard_map/all_gather | solution.py:197
  398.9 25.2 %conditional.5 = (f32[147456]{0:T(1024)S(1)}) conditional(s32[]{:T(128)} %convert_element_type.102, () %tuple.41, f32[13824,128]{1,0:T(8,128)} %all-gather.5.cloned.1.call-done), branch_computations={%region_25.0_spmd, %region_26.28_spmd} | conditional | flops 10196287488 | bytes 24772644 | solution.py:203
  424.9 50.1 %conditional.4 = (f32[442368]{0:T(1024)S(1)}) conditional(s32[]{:T(128)} %convert_element_type.102, () %tuple.40, f32[13824,128]{1,0:T(8,128)} %all-gather.5.cloned.1.call-done), branch_computations={%region_22.0_spmd, %region_23.25_spmd} | conditional | flops 23789666304 | bytes 50724900 | solution.py:203
  468.6 4.5 convolution_add_fusion
  476.2 76.1 %conditional.7 = (f32[589824]{0:T(1024)S(1)}) conditional(s32[]{:T(128)} %convert_element_type.102, () %tuple.43, f32[13824,128]{1,0:T(8,128)} %all-gather.5.cloned.1.call-done), branch_computations={%region_31.32_spmd, %region_32.34_spmd} | conditional | flops 30598152192 | bytes 141557856 | solution.py:203
  495.7 5.3 fusion.98
  503.0 9.1 %fusion.32 = f32[384,384]{1,0:T(8,128)S(1)} fusion(f32[384,1536]{1,0:T(8,128)} %fusion.98, f32[1536,384]{0,1:T(8,128)} %copy.25), kind=kOutput, calls=%fused_computation.85 | convolution fusion | flops 2719088640 | bytes 5308416 | tf_op jit(solution)/shard_map/cond/branch_1_fun/dot_general | solution.py:79
  536.8 4.7 fusion.19
  542.8 4.9 convolution_add_fusion.15
  553.7 58.4 %conditional.6 = (f32[589824]{0:T(1024)}) conditional(s32[]{:T(128)} %convert_element_type.102, () %tuple.42, f32[13824,128]{1,0:T(8,128)} %all-gather.5.cloned.1.call-done), branch_computations={%region_28.0_spmd, %region_29.31_spmd} | conditional | flops 30586355712 | bytes 63701028 | solution.py:203
  572.2 4.5 fusion.93
  612.2 7.3 maximum_bitcast_fusion.1
  627.8 37.0 %psum.7 = f32[36,128]{1,0:T(8,128)S(1)} all-reduce(f32[36,128]{1,0:T(8,128)S(1)} %bitcast.231), channel_id=1, replica_groups=mesh['dp'=32] {'dp'}, use_global_device_ids=true, to_apply=%region_21.0 | all-reduce | flops 4608 | bytes 36864 | tf_op jit(solution)/shard_map/psum | solution.py:194
  665.4 5.7 add_convert_fusion.1
  671.1 63.5 %reduce-scatter.5.cloned.1.call-done = f32[432,128]{1,0:T(8,128)} async-done(((f32[13824,128]{1,0:T(8,128)}), f32[432,128]{1,0:T(8,128)}) %reduce-scatter.5.cloned.1.call-update) | async-done | bytes 221200 | tf_op jit(solution)/shard_map/reduce_scatter | solution.py:208
  (234 shorter events, 271.7 us)
Async XLA Ops:
  7.2 66.5 %all-gather.3.cloned.1.call-start = ((), (), s32[]{:S(2)}) async-start(), calls=%async_computation.2 | async-start | bytes 3649536 | tf_op jit(solution)/shard_map/all_gather | solution.py:92
  7.9 315.4 %reduce-scatter.3.cloned.1.call-start = ((), (), s32[]{:S(2)}) async-start(), calls=%async_computation.3 | async-start | bytes 7299072 | tf_op jit(solution)/shard_map/reduce_scatter | solution.py:195
  78.7 3.6 copy-start.3
  78.7 3.6 copy-start.30
  78.7 3.6 copy-start.34
  99.8 7.6 %copy-start.10 = (bf16[5,197,1,6,64]{1,4,3,0,2:T(8,128)(2,1)}, bf16[5,197,1,6,64]{1,4,3,0,2:T(8,128)(2,1)S(1)}, u32[]{:S(2)}) copy-start(bf16[5,197,1,6,64]{1,4,3,0,2:T(8,128)(2,1)S(1)} %copy.51) | copy-start | bytes 2269444
  115.3 25.2 %copy-start.4 = (f32[985,384]{1,0:T(8,128)}, f32[985,384]{1,0:T(8,128)S(1)}, u32[]{:S(2)}) copy-start(f32[985,384]{1,0:T(8,128)S(1)} %get-tuple-element.75) | copy-start | bytes 4538884
  115.7 15.7 %copy-start.19 = (bf16[985,384]{1,0:T(8,128)(2,1)S(1)}, bf16[985,384]{1,0:T(8,128)(2,1)}, u32[]{:S(2)}) copy-start(bf16[985,384]{1,0:T(8,128)(2,1)} %param.17) | copy-start | bytes 2269444
  115.7 15.7 %copy-start.23 = (bf16[1536,384]{1,0:T(8,128)(2,1)S(1)}, bf16[1536,384]{1,0:T(8,128)(2,1)}, u32[]{:S(2)}) copy-start(bf16[1536,384]{1,0:T(8,128)(2,1)} %reshape.253) | copy-start | bytes 3538948
  146.1 9.2 %slice-start = ((s8[6144000]{0:T(1024)(128)(4,1)}), s8[1949696]{0:T(1024)(128)(4,1)S(1)}, s32[]{:S(2)}) async-start(s8[6144000]{0:T(1024)(128)(4,1)} %bitcast.229), calls=%async_computation.6 | async-start | bytes 3899392
  149.9 5.4 slice-start.1
  149.9 5.4 copy-start.15
  149.9 5.4 copy-start.16
  181.7 7.6 %copy-start.35 = (f32[384]{0:T(512)S(1)}, f32[384]{0:T(512)}, u32[]{:S(2)}) copy-start(f32[384]{0:T(512)} %get-tuple-element.70) | copy-start | bytes 4612
  205.0 118.2 %copy-start.25 = (f32[432,128]{1,0:T(8,128)S(1)}, f32[432,128]{1,0:T(8,128)}, u32[]{:S(2)}) copy-start(f32[432,128]{1,0:T(8,128)} %param.18) | copy-start | bytes 663556
  205.1 193.8 %all-gather.5.cloned.1.call-start = ((), (), s32[]{:S(2)}) async-start(), calls=%async_computation.4 | async-start | bytes 7299072 | tf_op jit(solution)/shard_map/all_gather | solution.py:197
  324.9 409.7 %reduce-scatter.5.cloned.1.call-start = ((), (), s32[]{:S(2)}) async-start(), calls=%async_computation.5 | async-start | bytes 7299072 | tf_op jit(solution)/shard_map/reduce_scatter | solution.py:208
  503.0 10.4 %copy-start.1 = (f32[384,1536]{1,0:T(8,128)S(1)}, f32[384,1536]{1,0:T(8,128)}, u32[]{:S(2)}) copy-start(f32[384,1536]{1,0:T(8,128)} %fusion.98) | copy-start | bytes 7077892 | tf_op jit(solution)/shard_map/cond
  503.0 10.4 %copy-start.2 = (f32[1536,384]{0,1:T(8,128)S(1)}, f32[1536,384]{0,1:T(8,128)}, u32[]{:S(2)}) copy-start(f32[1536,384]{0,1:T(8,128)} %copy.25) | copy-start | bytes 7077892 | tf_op jit(solution)/shard_map/cond
  536.8 6.1 copy-start.9
  625.9 38.9 %copy-start.29 = (f32[36,128]{1,0:T(8,128)S(1)}, f32[36,128]{1,0:T(8,128)}, u32[]{:S(2)}) copy-start(f32[36,128]{1,0:T(8,128)} %param.19) | copy-start | bytes 55300
  625.9 39.5 %copy-start.5 = (f32[985,384]{1,0:T(8,128)S(1)}, f32[985,384]{1,0:T(8,128)}, u32[]{:S(2)}) copy-start(f32[985,384]{1,0:T(8,128)} %copy-done.4) | copy-start | bytes 4538884
  625.9 39.5 %copy-start.33 = (f32[384]{0:T(512)S(1)}, f32[384]{0:T(512)}, u32[]{:S(2)}) copy-start(f32[384]{0:T(512)} %get-tuple-element.64) | copy-start | bytes 4612
  664.8 6.3 copy-start.26
  (21 other events, 35.3 us)
Sparse Core Ops, SparseCore 0:
  10.9 62.7 all-gather.2
  205.2 118.0 reduce-scatter.2
  327.2 71.6 all-gather.4
  619.6 114.9 reduce-scatter.4
where the time goes:
time: 752 us; the launch traced here: 743 us
  waiting for transfers between devices  315 us (42%)
  matrix products  223 us (30%)
  local copies, waits for them, and re-layouts  93.4 us (12%)
  other arithmetic  54.2 us (7%)
  blocking collectives  37 us (5%)
  between operations  14.8 us (2%)
    reduce_scatter x1, waiting for transfers between devices, on_device(): lax.psum_scatter(local_grads, 'dp', scatter_dimension=0, tiled=True)  118 us
    all_gather x1, waiting for transfers between devices, on_device(): gathered = lax.all_gather(new_mom_weights, 'dp', axis=0, tiled=True)  73.9 us
    dot_general x20, matrix products, orthogonalize(): square = jnp.dot(current, current.T, precision=HIGH)  69.5 us
    dot_general x20, matrix products, orthogonalize(): current = first * current + jnp.dot(poly, current, precision=HIGH)  66.7 us
    reduce_scatter x1, waiting for transfers between devices, on_device(): lax.psum_scatter(owned_flat, 'dp', scatter_dimension=0, tiled=True)  63.5 us
    all_gather x1, waiting for transfers between devices, on_device(): whole = lax.all_gather(weights, 'dp', axis=0, tiled=True)  58.9 us
    psum x1, blocking collectives, on_device(): grad_vectors = lax.psum(local_vector_grads, 'dp')  37 us
    dot_general x20, matrix products, orthogonalize(): poly = second * square + third * jnp.dot(square, square, precision=HIGH)  26.1 us
  transfers between devices with their start and end apart: 4, of which 4 were waited for; matrix products, arithmetic and copies ran while one was open for 2% of the time, Pallas kernels for 0%

commit v1 on v0

--- a/solution.py
+++ b/solution.py
@@ -191,7 +191,8 @@
             grad_bias_up,
         ]
     ).reshape(-1, 128)
-    grad_vectors = lax.psum(local_vector_grads, "dp")
+    parts = lax.all_gather(local_vector_grads, "dp", axis=0, tiled=False)
+    grad_vectors = parts.sum(axis=0)
     grad_weights = lax.psum_scatter(local_grads, "dp", scatter_dimension=0, tiled=True)
     new_mom_weights = MOMENTUM * mom_weights + grad_weights
     gathered = lax.all_gather(new_mom_weights, "dp", axis=0, tiled=True)

time: 752 us -> 752 us (level)
    all_gather x0 -> x1, blocking collectives: none -> 38.1 us  [on_device(): parts = lax.all_gather(local_vector_grads, 'dp', axis=0, tiled=False)]
    psum x1 -> x0, blocking collectives: 37 us -> none  [on_device(): grad_vectors = lax.psum(local_vector_grads, 'dp')]
where the time goes in v1:
time: 752 us; the launch traced here: 743 us
  waiting for transfers between devices  314 us (42%)
  matrix products  222 us (30%)
  local copies, waits for them, and re-layouts  93.4 us (12%)
  other arithmetic  54.3 us (7%)
  blocking collectives  38.1 us (5%)
  between operations  14.8 us (2%)
    reduce_scatter x1, waiting for transfers between devices, on_device(): lax.psum_scatter(local_grads, 'dp', scatter_dimension=0, tiled=True)  118 us
    all_gather x1, waiting for transfers between devices, on_device(): gathered = lax.all_gather(new_mom_weights, 'dp', axis=0, tiled=True)  73.9 us
    dot_general x20, matrix products, orthogonalize(): square = jnp.dot(current, current.T, precision=HIGH)  69.5 us
    dot_general x20, matrix products, orthogonalize(): current = first * current + jnp.dot(poly, current, precision=HIGH)  66.7 us
    reduce_scatter x1, waiting for transfers between devices, on_device(): lax.psum_scatter(owned_flat, 'dp', scatter_dimension=0, tiled=True)  62.8 us
    all_gather x1, waiting for transfers between devices, on_device(): whole = lax.all_gather(weights, 'dp', axis=0, tiled=True)  58.9 us
    all_gather x1, blocking collectives, on_device(): parts = lax.all_gather(local_vector_grads, 'dp', axis=0, tiled=False)  38.1 us
    dot_general x20, matrix products, orthogonalize(): poly = second * square + third * jnp.dot(square, square, precision=HIGH)  26.1 us
  transfers between devices with their start and end apart: 4, of which 4 were waited for; matrix products, arithmetic and copies ran while one was open for 2% of the time, Pallas kernels for 0%

profile of v1, /device:TPU:0, one launch (start us, length us, event | category | flops | bytes accessed | tf_op | source)
XLA Modules:
  0.0 743.2 jit_solution(17653688732029494299)
XLA Ops:
  14.8 58.9 %all-gather.3.cloned.1.call-done = bf16[13824,128]{1,0:T(8,128)(2,1)} async-done(((bf16[432,128]{1,0:T(8,128)(2,1)}), bf16[13824,128]{1,0:T(8,128)(2,1)}) %all-gather.3.cloned.1.call-update) | async-done | bytes 3538960 | tf_op jit(solution)/shard_map/all_gather | solution.py:92
  85.0 5.7 reshape.258
  90.7 5.8 fusion.79
  115.7 15.7 %multiply_convert_fusion.1 = (bf16[985,1536]{1,0:T(8,128)(2,1)}, f32[985,1536]{1,0:T(8,128)S(1)}, f32[985,1536]{1,0:T(8,128)S(1)}) fusion(f32[1536]{0:T(1024)S(1)} %copy-done.31, bf16[384,1536]{1,0:T(8,128)(2,1)S(1)} %copy-done.24, f32[985,384]{1,0:T(8,128)S(1)} %get-tuple-element.75, f32[384]{0:T(512)S(1)} %copy-done.36, f32[384]{0:T(512)S(1)} %get-tuple-element.66, ...), kind=kOutput, calls=%fused_computation.96 | convolution fusion | flops 1263699840 | bytes 17839304 | tf_op jit(solution)/shard_map/dot_general | solution.py:54
  149.9 5.4 convolution_bitcast_fusion
  177.2 4.5 copy.57
  181.7 7.6 %convert_element_type.97 = bf16[985,1152]{0,1:T(8,128)(2,1)} reshape(bf16[5,197,3,6,64]{1,0,4,3,2:T(8,128)(2,1)} %copy.57) | data formatting | bytes 4538880 | tf_op jit(solution)/shard_map/convert_element_type | solution.py:168
  196.2 8.8 %maximum_bitcast_fusion = f32[13824,128]{1,0:T(8,128)} fusion(f32[589824]{0:T(1024)S(1)} %reshape.255, f32[589824]{0:T(1024)} %reshape.254, f32[147456]{0:T(1024)} %reshape.253, f32[442368]{0:T(1024)} %reshape.252), kind=kLoop, calls=%fused_computation.87 | loop fusion | flops 5308416 | bytes 14155776 | tf_op jit(solution)/shard_map/reshape | solution.py:180
  205.1 118.2 %reduce-scatter.3.cloned.1.call-done = f32[432,128]{1,0:T(8,128)} async-done(((f32[13824,128]{1,0:T(8,128)}), f32[432,128]{1,0:T(8,128)}) %reduce-scatter.3.cloned.1.call-update) | async-done | bytes 221200 | tf_op jit(solution)/shard_map/reduce_scatter | solution.py:196
  325.0 73.9 %all-gather.5.cloned.1.call-done = f32[13824,128]{1,0:T(8,128)} async-done(((f32[432,128]{1,0:T(8,128)}), f32[13824,128]{1,0:T(8,128)}) %all-gather.5.cloned.1.call-update) | async-done | bytes 7077904 | tf_op jit(solution)/shard_map/all_gather | solution.py:198
  398.9 25.2 %conditional.5 = (f32[147456]{0:T(1024)S(1)}) conditional(s32[]{:T(128)} %convert_element_type.102, () %tuple.41, f32[13824,128]{1,0:T(8,128)} %all-gather.5.cloned.1.call-done), branch_computations={%region_25.0_spmd, %region_26.28_spmd} | conditional | flops 10196287488 | bytes 24772644 | solution.py:204
  424.9 50.1 %conditional.4 = (f32[442368]{0:T(1024)S(1)}) conditional(s32[]{:T(128)} %convert_element_type.102, () %tuple.40, f32[13824,128]{1,0:T(8,128)} %all-gather.5.cloned.1.call-done), branch_computations={%region_22.0_spmd, %region_23.25_spmd} | conditional | flops 23789666304 | bytes 50724900 | solution.py:204
  468.6 4.5 convolution_add_fusion
  476.2 76.1 %conditional.7 = (f32[589824]{0:T(1024)S(1)}) conditional(s32[]{:T(128)} %convert_element_type.102, () %tuple.43, f32[13824,128]{1,0:T(8,128)} %all-gather.5.cloned.1.call-done), branch_computations={%region_31.32_spmd, %region_32.34_spmd} | conditional | flops 30598152192 | bytes 141557856 | solution.py:204
  495.7 5.3 fusion.98
  503.0 9.1 %fusion.32 = f32[384,384]{1,0:T(8,128)S(1)} fusion(f32[384,1536]{1,0:T(8,128)} %fusion.98, f32[1536,384]{0,1:T(8,128)} %copy.42), kind=kOutput, calls=%fused_computation.85 | convolution fusion | flops 2719088640 | bytes 5308416 | tf_op jit(solution)/shard_map/cond/branch_1_fun/dot_general | solution.py:79
  536.8 4.7 fusion.19
  542.8 4.9 convolution_add_fusion.15
  553.7 58.4 %conditional.6 = (f32[589824]{0:T(1024)}) conditional(s32[]{:T(128)} %convert_element_type.102, () %tuple.42, f32[13824,128]{1,0:T(8,128)} %all-gather.5.cloned.1.call-done), branch_computations={%region_28.0_spmd, %region_29.31_spmd} | conditional | flops 30586355712 | bytes 63701028 | solution.py:204
  572.2 4.5 fusion.93
  612.2 7.3 maximum_bitcast_fusion.1
  627.8 38.1 %all_gather.15 = f32[32,36,128]{2,1,0:T(8,128)S(1)} all-gather(f32[1,36,128]{2,1,0:T(8,128)S(1)} %bitcast.231), channel_id=1, replica_groups=mesh['dp'=32] {'dp'}, dimensions={0}, use_global_device_ids=true | all-gather | bytes 608256 | tf_op jit(solution)/shard_map/all_gather | solution.py:194
  666.5 5.2 add_convert_fusion.1
  671.8 62.8 %reduce-scatter.5.cloned.1.call-done = f32[432,128]{1,0:T(8,128)} async-done(((f32[13824,128]{1,0:T(8,128)}), f32[432,128]{1,0:T(8,128)}) %reduce-scatter.5.cloned.1.call-update) | async-done | bytes 221200 | tf_op jit(solution)/shard_map/reduce_scatter | solution.py:209
  (235 shorter events, 271.8 us)
Async XLA Ops:
  7.2 66.5 %all-gather.3.cloned.1.call-start = ((), (), s32[]{:S(2)}) async-start(), calls=%async_computation.2 | async-start | bytes 3649536 | tf_op jit(solution)/shard_map/all_gather | solution.py:92
  7.9 315.4 %reduce-scatter.3.cloned.1.call-start = ((), (), s32[]{:S(2)}) async-start(), calls=%async_computation.3 | async-start | bytes 7299072 | tf_op jit(solution)/shard_map/reduce_scatter | solution.py:196
  78.7 3.6 copy-start.3
  78.7 3.6 copy-start.30
  78.7 3.6 copy-start.34
  99.8 7.6 %copy-start.10 = (bf16[5,197,1,6,64]{1,4,3,0,2:T(8,128)(2,1)}, bf16[5,197,1,6,64]{1,4,3,0,2:T(8,128)(2,1)S(1)}, u32[]{:S(2)}) copy-start(bf16[5,197,1,6,64]{1,4,3,0,2:T(8,128)(2,1)S(1)} %copy.68) | copy-start | bytes 2269444
  115.3 25.2 %copy-start.4 = (f32[985,384]{1,0:T(8,128)}, f32[985,384]{1,0:T(8,128)S(1)}, u32[]{:S(2)}) copy-start(f32[985,384]{1,0:T(8,128)S(1)} %get-tuple-element.75) | copy-start | bytes 4538884
  115.7 15.7 %copy-start.19 = (bf16[985,384]{1,0:T(8,128)(2,1)S(1)}, bf16[985,384]{1,0:T(8,128)(2,1)}, u32[]{:S(2)}) copy-start(bf16[985,384]{1,0:T(8,128)(2,1)} %param.17) | copy-start | bytes 2269444
  115.7 15.7 %copy-start.23 = (bf16[1536,384]{1,0:T(8,128)(2,1)S(1)}, bf16[1536,384]{1,0:T(8,128)(2,1)}, u32[]{:S(2)}) copy-start(bf16[1536,384]{1,0:T(8,128)(2,1)} %reshape.250) | copy-start | bytes 3538948
  146.1 9.2 %slice-start = ((s8[6144000]{0:T(1024)(128)(4,1)}), s8[1949696]{0:T(1024)(128)(4,1)S(1)}, s32[]{:S(2)}) async-start(s8[6144000]{0:T(1024)(128)(4,1)} %bitcast.229), calls=%async_computation.6 | async-start | bytes 3899392
  149.9 5.4 slice-start.1
  149.9 5.4 copy-start.15
  149.9 5.4 copy-start.16
  181.7 7.6 %copy-start.35 = (f32[384]{0:T(512)S(1)}, f32[384]{0:T(512)}, u32[]{:S(2)}) copy-start(f32[384]{0:T(512)} %get-tuple-element.70) | copy-start | bytes 4612
  205.0 118.2 %copy-start.25 = (f32[432,128]{1,0:T(8,128)S(1)}, f32[432,128]{1,0:T(8,128)}, u32[]{:S(2)}) copy-start(f32[432,128]{1,0:T(8,128)} %param.18) | copy-start | bytes 663556
  205.1 193.8 %all-gather.5.cloned.1.call-start = ((), (), s32[]{:S(2)}) async-start(), calls=%async_computation.4 | async-start | bytes 7299072 | tf_op jit(solution)/shard_map/all_gather | solution.py:198
  324.9 409.6 %reduce-scatter.5.cloned.1.call-start = ((), (), s32[]{:S(2)}) async-start(), calls=%async_computation.5 | async-start | bytes 7299072 | tf_op jit(solution)/shard_map/reduce_scatter | solution.py:209
  503.0 10.4 %copy-start.1 = (f32[384,1536]{1,0:T(8,128)S(1)}, f32[384,1536]{1,0:T(8,128)}, u32[]{:S(2)}) copy-start(f32[384,1536]{1,0:T(8,128)} %fusion.98) | copy-start | bytes 7077892 | tf_op jit(solution)/shard_map/cond
  503.0 10.4 %copy-start.2 = (f32[1536,384]{0,1:T(8,128)S(1)}, f32[1536,384]{0,1:T(8,128)}, u32[]{:S(2)}) copy-start(f32[1536,384]{0,1:T(8,128)} %copy.42) | copy-start | bytes 7077892 | tf_op jit(solution)/shard_map/cond
  536.8 6.1 copy-start.9
  625.9 40.0 %copy-start.29 = (f32[36,128]{1,0:T(8,128)S(1)}, f32[36,128]{1,0:T(8,128)}, u32[]{:S(2)}) copy-start(f32[36,128]{1,0:T(8,128)} %param.19) | copy-start | bytes 55300
  625.9 40.6 %copy-start.5 = (f32[985,384]{1,0:T(8,128)S(1)}, f32[985,384]{1,0:T(8,128)}, u32[]{:S(2)}) copy-start(f32[985,384]{1,0:T(8,128)} %copy-done.4) | copy-start | bytes 4538884
  625.9 40.6 %copy-start.33 = (f32[384]{0:T(512)S(1)}, f32[384]{0:T(512)}, u32[]{:S(2)}) copy-start(f32[384]{0:T(512)} %get-tuple-element.64) | copy-start | bytes 4612
  665.9 5.9 copy-start.26
  (21 other events, 35.3 us)
Sparse Core Ops, SparseCore 0:
  10.9 62.7 all-gather.2
  205.2 118.0 reduce-scatter.2
  327.2 71.6 all-gather.4
  619.6 114.9 reduce-scatter.4
